TPU v7x, 128 devices: a whole 4x4x4 slice. The times are simulated.
128 devices in a mesh: ctx: 32 (over y, z_hi, x), tp: 4 (over z_lo, core).
Axes of the slice: x: 4, y: 4, z: 4 (z_hi: 2, z_lo: 2; z = z_hi * 2 + z_lo), core: 2. Of those that a mesh axis runs over, the one named last changes fastest.
Arguments:
- query_rot: bfloat16 [16384, 3072], P('ctx', 'tp'), may hold values from -12 to 12
- key_rot: bfloat16 [16384, 3072], P('ctx', 'tp'), may hold values from -12 to 12
- value: bfloat16 [16384, 3072], P('ctx', 'tp'), may hold values from -6 to 6
- grad_out: bfloat16 [16384, 3072], P('ctx', 'tp'), may hold values from -6 to 6
- text_key: bfloat16 [256, 3072], P('ctx', 'tp'), may hold values from -6 to 6
- text_value: bfloat16 [256, 3072], P('ctx', 'tp'), may hold values from -6 to 6
- positions: int32 [3, 16384], P(None, 'ctx'), may hold values from 0 to 63, as said below
- tile_mask: int32 [128, 128], replicated, may hold values from 0 to 1, as said below
Outputs:
- grad_query: bfloat16 [16384, 3072], P('ctx', 'tp')
- grad_key: bfloat16 [16384, 3072], P('ctx', 'tp')
- grad_value: bfloat16 [16384, 3072], P('ctx', 'tp')
- grad_text_key: bfloat16 [256, 3072], P('ctx', 'tp')
- grad_text_value: bfloat16 [256, 3072], P('ctx', 'tp')
Inputs may be any that keep to these rules, and one draw needn't show every extreme that they name: tile_mask[a, b] is 1 when tiles a and b lie in the same frame (2 tiles a frame, in token order) and 0 when their frames are more than 2 apart. positions[0, n] is n // 256; positions[1, n] and positions[2, n] are the row and column of token n in its frame of rows of 16 tokens, each plus an offset of 0 to 31 common to all tokens.
All inputs are finite; a program needn't handle non-finite values.
Results may differ from a plain program's by a relative error of at most 0.02.
Values may be sent and summed in bfloat16 or wider, within the bound.
No kernel may reach another device: no remote copies, remote signals or barrier semaphores. Data moves between devices by JAX's collectives and lax.ppermute only.
A program may use at most 128 MiB of HBM per device.

v0:
```python
import jax
import jax.numpy as jnp
from jax import lax
from jax.sharding import PartitionSpec as P

D_HEAD = 128
TILE = 128
ROPE_THETA = 256.0
TIME_STRETCH = 0.25


def shifted(block, axis, distance):
    devices = range(lax.axis_size(axis))
    route = [(i - distance, i) for i in devices if i - distance in devices]
    return lax.ppermute(block, axis, route)


def rope_tables(positions, head_dim):
    time_dims = head_dim // 8
    plane_dims = (head_dim - time_dims) // 2
    layout = ((time_dims, TIME_STRETCH), (plane_dims, 1.0), (plane_dims, 1.0))
    angle_parts = []
    for axis_id in range(3):
        seg_width, stretch = layout[axis_id]
        pair_ids = jnp.arange(seg_width // 2, dtype=jnp.float32)
        frequency = ROPE_THETA ** (-2.0 * pair_ids / seg_width)
        scaled_pos = positions[axis_id].astype(jnp.float32) * stretch
        angle_parts.append(scaled_pos[:, None] * frequency[None, :])
    angles = jnp.concatenate(angle_parts, axis=1)
    return (jnp.cos(angles), jnp.sin(angles))


def unrotate(grad_rot, cosine, sine):
    tok_rows = grad_rot.shape[0]
    pairs = grad_rot.reshape(tok_rows, -1, cosine.shape[1], 2)
    even_part = pairs[..., 0]
    odd_part = pairs[..., 1]
    cos_rows = cosine[:, None, :]
    sin_rows = sine[:, None, :]
    turned = jnp.stack(
        [cos_rows * even_part + sin_rows * odd_part, cos_rows * odd_part - sin_rows * even_part],
        axis=-1,
    )
    return turned.reshape(grad_rot.shape)


def scores_of(query_head, key_head):
    return jnp.einsum(
        "qd,kd->qk", query_head, key_head, preferred_element_type=jnp.float32
    ) * D_HEAD ** (-0.5)


def piece_grads(query_head, grad_head, weights, row_delta, key_head, value_head):
    score_scale = D_HEAD ** (-0.5)
    dprobs = jnp.einsum("qd,kd->qk", grad_head, value_head, preferred_element_type=jnp.float32)
    dscores = (weights.astype(jnp.float32) * (dprobs - row_delta[:, None])).astype(jnp.bfloat16)
    results = []
    results.append(jnp.dot(dscores, key_head, preferred_element_type=jnp.float32) * score_scale)
    results.append(
        jnp.einsum("qk,qd->kd", dscores, query_head, preferred_element_type=jnp.float32)
        * score_scale
    )
    results.append(jnp.einsum("qk,qd->kd", weights, grad_head, preferred_element_type=jnp.float32))
    return tuple(results)


def shards(query_rot, key_rot, value, grad_out, text_key, text_value, positions, tile_mask):
    tok_rows = query_rot.shape[0]
    head_count = query_rot.shape[1] // D_HEAD
    tile_rows = tok_rows // TILE
    ctx_index = lax.axis_index("ctx")
    text_keys, text_values = (
        lax.all_gather(text_key, "ctx", axis=0, tiled=True),
        lax.all_gather(text_value, "ctx", axis=0, tiled=True),
    )
    left_keys, left_values = shifted((key_rot, value), "ctx", 1)
    right_keys, right_values = shifted((key_rot, value), "ctx", -1)
    padded_mask = jnp.pad(tile_mask, ((tile_rows, tile_rows), (tile_rows, tile_rows)))

    def window(col_shift):
        mask_block = lax.dynamic_slice(
            padded_mask,
            ((ctx_index + 1) * tile_rows, (ctx_index + col_shift + 1) * tile_rows),
            (tile_rows, tile_rows),
        )
        return jnp.repeat(jnp.repeat(mask_block, TILE, axis=0), TILE, axis=1) > 0

    allow_left = window(-1)
    allow_own = window(0)
    allow_right = window(1)
    query_parts, own_key_parts, own_value_parts = ([], [], [])
    left_key_parts, left_value_parts, right_key_parts, right_value_parts = ([], [], [], [])
    text_key_parts, text_value_parts, total_parts, delta_parts = ([], [], [], [])
    for head_id in range(head_count):
        head_cols = slice(head_id * D_HEAD, (head_id + 1) * D_HEAD)
        query_head = query_rot[:, head_cols]
        grad_head = grad_out[:, head_cols]
        text_key_head = text_keys[:, head_cols]
        text_value_head = text_values[:, head_cols]
        sides = (
            (left_keys[:, head_cols], left_values[:, head_cols], allow_left),
            (key_rot[:, head_cols], value[:, head_cols], allow_own),
            (right_keys[:, head_cols], right_values[:, head_cols], allow_right),
        )
        masked = []
        for key_head, value_head, allowed in sides:
            masked.append(jnp.where(allowed, scores_of(query_head, key_head), -jnp.inf))
        text_scores = scores_of(query_head, text_key_head)
        row_max = jnp.max(text_scores, axis=1)
        for piece_scores in masked:
            row_max = jnp.maximum(row_max, jnp.max(piece_scores, axis=1))
        row_total = jnp.sum(jnp.exp(text_scores - row_max[:, None]), axis=1)
        for piece_scores in masked:
            row_total = row_total + jnp.sum(jnp.exp(piece_scores - row_max[:, None]), axis=1)
        log_total = row_max + jnp.log(row_total)
        weight_list = [
            jnp.exp(piece_scores - log_total[:, None]).astype(jnp.bfloat16)
            for piece_scores in masked
        ]
        text_weights = jnp.exp(text_scores - log_total[:, None]).astype(jnp.bfloat16)
        attended = jnp.dot(text_weights, text_value_head, preferred_element_type=jnp.float32)
        for slot in range(3):
            attended = attended + jnp.dot(
                weight_list[slot], sides[slot][1], preferred_element_type=jnp.float32
            )
        row_delta = jnp.sum(grad_head.astype(jnp.float32) * attended, axis=1)
        total_parts.append(log_total)
        delta_parts.append(row_delta)
        text_terms = piece_grads(
            query_head, grad_head, text_weights, row_delta, text_key_head, text_value_head
        )
        query_grad = text_terms[0]
        text_key_parts.append(text_terms[1])
        text_value_parts.append(text_terms[2])
        for slot in range(3):
            key_head, value_head, allowed = sides[slot]
            terms = piece_grads(
                query_head, grad_head, weight_list[slot], row_delta, key_head, value_head
            )
            query_grad = query_grad + terms[0]
            if slot == 0:
                left_key_parts.append(terms[1])
                left_value_parts.append(terms[2])
            if slot == 1:
                own_key_parts.append(terms[1])
                own_value_parts.append(terms[2])
            if slot == 2:
                right_key_parts.append(terms[1])
                right_value_parts.append(terms[2])
        query_parts.append(query_grad)
    query_grad_all = jnp.concatenate(query_parts, axis=1)
    key_grad_all = jnp.concatenate(own_key_parts, axis=1)
    value_grad_all = jnp.concatenate(own_value_parts, axis=1)
    right_back = (
        shifted(jnp.concatenate(left_key_parts, axis=1).astype(jnp.bfloat16), "ctx", -1).astype(
            jnp.float32
        ),
        shifted(jnp.concatenate(left_value_parts, axis=1).astype(jnp.bfloat16), "ctx", -1).astype(
            jnp.float32
        ),
    )
    left_back = (
        shifted(jnp.concatenate(right_key_parts, axis=1).astype(jnp.bfloat16), "ctx", 1).astype(
            jnp.float32
        ),
        shifted(jnp.concatenate(right_value_parts, axis=1).astype(jnp.bfloat16), "ctx", 1).astype(
            jnp.float32
        ),
    )
    key_grad_all = key_grad_all + right_back[0] + left_back[0]
    value_grad_all = value_grad_all + right_back[1] + left_back[1]
    text_key_grad, text_value_grad = (
        lax.psum_scatter(
            jnp.concatenate(text_key_parts, axis=1).astype(jnp.bfloat16),
            "ctx",
            scatter_dimension=0,
            tiled=True,
        ).astype(jnp.float32),
        lax.psum_scatter(
            jnp.concatenate(text_value_parts, axis=1).astype(jnp.bfloat16),
            "ctx",
            scatter_dimension=0,
            tiled=True,
        ).astype(jnp.float32),
    )
    cosine, sine = rope_tables(positions, D_HEAD)
    grad_query = unrotate(query_grad_all, cosine, sine).astype(jnp.bfloat16)
    grad_key = unrotate(key_grad_all, cosine, sine).astype(jnp.bfloat16)
    return (
        grad_query,
        grad_key,
        value_grad_all.astype(jnp.bfloat16),
        text_key_grad.astype(jnp.bfloat16),
        text_value_grad.astype(jnp.bfloat16),
    )


def solution(mesh):
    placed = (
        P("ctx", "tp"),
        P("ctx", "tp"),
        P("ctx", "tp"),
        P("ctx", "tp"),
        P("ctx", "tp"),
        P("ctx", "tp"),
        P(None, "ctx"),
        P(),
    )
    return jax.shard_map(
        shards,
        mesh=mesh,
        in_specs=placed,
        out_specs=(P("ctx", "tp"), P("ctx", "tp"), P("ctx", "tp"), P("ctx", "tp"), P("ctx", "tp")),
        check_vma=False,
    )
```

profile of v0, /device:TPU:0, one launch (start us, length us, event | category | flops | bytes accessed | tf_op | source)
XLA Modules:
  0.0 775.8 jit_solution(6786113106563927850)
XLA Ops:
  8.7 5.5 collective-permute-start
  14.2 3.5 collective-permute-start.2
  18.9 118.4 %all_gather.6 = bf16[256,768]{1,0:T(8,128)(2,1)S(1)} all-gather(bf16[8,768]{1,0:T(8,128)(2,1)} %param.12), channel_id=1, replica_groups=mesh['ctx'=32,'tp'=4] {'ctx'}, dimensions={0}, use_global_device_ids=true | all-gather | bytes 405504 | tf_op jit(solution)/shard_map/all_gather | solution.py:73
  137.3 1.9 fusion.352
  144.5 94.3 %all_gather.7 = bf16[256,768]{1,0:T(8,128)(2,1)} all-gather(bf16[8,768]{1,0:T(8,128)(2,1)S(1)} %copy-done.75), channel_id=1, replica_groups=mesh['ctx'=32,'tp'=4] {'ctx'}, dimensions={0}, use_global_device_ids=true | all-gather | bytes 405504 | tf_op jit(solution)/shard_map/all_gather | solution.py:74
  241.1 1.9 fusion.351
  243.0 1.9 fusion.347
  244.9 1.8 fusion.343
  246.7 1.9 fusion.355
  250.3 2.2 fusion.363
  325.4 1.9 copy.153
  328.6 1.9 fusion.130
  345.4 5.8 collective-permute-start.7
  395.6 2.2 reshape.347
  397.8 5.7 collective-permute-start.5
  403.6 2.2 fusion.50
  405.8 2.1 fusion.49
  408.9 1.8 add_convert_fusion
  412.5 3.3 convert_add_fusion
  415.8 2.3 reshape.348
  418.1 4.3 add_convert_fusion.1
  422.4 3.6 pad_maximum_fusion
  429.0 116.1 %reduce-scatter.9.cloned.1.call-done = bf16[8,768]{1,0:T(8,128)(2,1)} async-done(((bf16[256,768]{1,0:T(8,128)(2,1)}), bf16[8,768]{1,0:T(8,128)(2,1)}) %reduce-scatter.9.cloned.1.call-update) | async-done | bytes 12304
  545.0 223.7 %reduce-scatter.7.cloned.1.call-done = bf16[8,768]{1,0:T(8,128)(2,1)} async-done(((bf16[256,768]{1,0:T(8,128)(2,1)}), bf16[8,768]{1,0:T(8,128)(2,1)}) %reduce-scatter.7.cloned.1.call-update) | async-done | bytes 12304
  (389 shorter events, 149.5 us)
Async XLA Ops:
  7.2 133.8 %copy-start.1 = (bf16[512,768]{1,0:T(8,128)(2,1)S(1)}, bf16[512,768]{1,0:T(8,128)(2,1)}, u32[]{:S(2)}) copy-start(bf16[512,768]{1,0:T(8,128)(2,1)} %param.8) | copy-start | bytes 2359300
  7.2 135.5 %copy-start.85 = (s32[3,512]{1,0:T(4,128)S(1)}, s32[3,512]{1,0:T(4,128)}, u32[]{:S(2)}) copy-start(s32[3,512]{1,0:T(4,128)} %param.14) | copy-start | bytes 18436
  7.2 135.5 %copy-start.69 = (s32[128,128]{1,0:T(8,128)S(1)}, s32[128,128]{1,0:T(8,128)}, u32[]{:S(2)}) copy-start(s32[128,128]{1,0:T(8,128)} %param.15) | copy-start | bytes 196612
  7.2 137.3 %copy-start.75 = (bf16[8,768]{1,0:T(8,128)(2,1)S(1)}, bf16[8,768]{1,0:T(8,128)(2,1)}, u32[]{:S(2)}) copy-start(bf16[8,768]{1,0:T(8,128)(2,1)} %param.13) | copy-start | bytes 36868
  7.2 231.6 %copy-start = (bf16[512,768]{1,0:T(8,128)(2,1)S(1)}, bf16[512,768]{1,0:T(8,128)(2,1)}, u32[]{:S(2)}) copy-start(bf16[512,768]{1,0:T(8,128)(2,1)} %param.11) | copy-start | bytes 2359300
  7.2 537.8 %reduce-scatter.9.cloned.1.call-start = ((), (), s32[]{:S(2)}) async-start(), calls=%async_computation.3 | async-start | bytes 405504
  7.3 256.0 %collective-permute-start.1 = (bf16[512,768]{1,0:T(8,128)(2,1)}, bf16[512,768]{1,0:T(8,128)(2,1)}, u32[]{:S(2)}, u32[]{:S(2)}) collective-permute-start(bf16[512,768]{1,0:T(8,128)(2,1)} %param.9), channel_id=1, source_target_pairs={{4,0},{8,4},{12,8},{16,12},{20,16},{24,20},{28,24},{32,28},{36,32}... | collective-permute-start | bytes 2359304 | tf_op jit(solution)/shard_map/ppermute | solution.py:15
  8.7 255.9 %collective-permute-start = (bf16[512,768]{1,0:T(8,128)(2,1)}, bf16[512,768]{1,0:T(8,128)(2,1)}, u32[]{:S(2)}, u32[]{:S(2)}) collective-permute-start(bf16[512,768]{1,0:T(8,128)(2,1)} %param.9), channel_id=1, source_target_pairs={{0,4},{4,8},{8,12},{12,16},{16,20},{20,24},{24,28},{28,32},{32,36}... | collective-permute-start | bytes 2359304 | tf_op jit(solution)/shard_map/ppermute | solution.py:15
  14.2 272.3 %collective-permute-start.2 = (bf16[512,768]{1,0:T(8,128)(2,1)}, bf16[512,768]{1,0:T(8,128)(2,1)}, u32[]{:S(2)}, u32[]{:S(2)}) collective-permute-start(bf16[512,768]{1,0:T(8,128)(2,1)} %param.10), channel_id=1, source_target_pairs={{0,4},{4,8},{8,12},{12,16},{16,20},{20,24},{24,28},{28,32},{32,36}... | collective-permute-start | bytes 2359304 | tf_op jit(solution)/shard_map/ppermute | solution.py:15
  17.6 272.4 %collective-permute-start.3 = (bf16[512,768]{1,0:T(8,128)(2,1)}, bf16[512,768]{1,0:T(8,128)(2,1)}, u32[]{:S(2)}, u32[]{:S(2)}) collective-permute-start(bf16[512,768]{1,0:T(8,128)(2,1)} %param.10), channel_id=1, source_target_pairs={{4,0},{8,4},{12,8},{16,12},{20,16},{24,20},{28,24},{32,28},{36,32}... | collective-permute-start | bytes 2359304 | tf_op jit(solution)/shard_map/ppermute | solution.py:15
  141.0 100.1 %copy-start.50 = (bf16[512,768]{1,0:T(8,128)(2,1)S(1)}, bf16[512,768]{1,0:T(8,128)(2,1)}, u32[]{:S(2)}) copy-start(bf16[512,768]{1,0:T(8,128)(2,1)} %param.9) | copy-start | bytes 2359300
  267.0 40.5 %copy-start.9 = (bf16[512,512]{0,1:T(8,128)(2,1)}, bf16[512,512]{0,1:T(8,128)(2,1)S(1)}, u32[]{:S(2)}) copy-start(bf16[512,512]{0,1:T(8,128)(2,1)S(1)} %get-tuple-element.71) | copy-start | bytes 1572868
  267.1 44.2 %copy-start.11 = (bf16[512,512]{0,1:T(8,128)(2,1)}, bf16[512,512]{0,1:T(8,128)(2,1)S(1)}, u32[]{:S(2)}) copy-start(bf16[512,512]{0,1:T(8,128)(2,1)S(1)} %get-tuple-element.70) | copy-start | bytes 1572868
  271.1 43.2 %copy-start.13 = (bf16[512,512]{0,1:T(8,128)(2,1)}, bf16[512,512]{0,1:T(8,128)(2,1)S(1)}, u32[]{:S(2)}) copy-start(bf16[512,512]{0,1:T(8,128)(2,1)S(1)} %get-tuple-element.74) | copy-start | bytes 1572868
  271.1 45.7 %copy-start.7 = (bf16[512,512]{0,1:T(8,128)(2,1)}, bf16[512,512]{0,1:T(8,128)(2,1)S(1)}, u32[]{:S(2)}) copy-start(bf16[512,512]{0,1:T(8,128)(2,1)S(1)} %get-tuple-element.72) | copy-start | bytes 1572868
  285.5 17.8 %copy-start.25 = (bf16[512,512]{0,1:T(8,128)(2,1)}, bf16[512,512]{0,1:T(8,128)(2,1)S(1)}, u32[]{:S(2)}) copy-start(bf16[512,512]{0,1:T(8,128)(2,1)S(1)} %get-tuple-element.68) | copy-start | bytes 1572868
  285.5 19.3 %copy-start.17 = (bf16[512,512]{0,1:T(8,128)(2,1)}, bf16[512,512]{0,1:T(8,128)(2,1)S(1)}, u32[]{:S(2)}) copy-start(bf16[512,512]{0,1:T(8,128)(2,1)S(1)} %get-tuple-element.66) | copy-start | bytes 1572868
  285.5 20.7 %copy-start.33 = (bf16[512,512]{0,1:T(8,128)(2,1)}, bf16[512,512]{0,1:T(8,128)(2,1)S(1)}, u32[]{:S(2)}) copy-start(bf16[512,512]{0,1:T(8,128)(2,1)S(1)} %get-tuple-element.67) | copy-start | bytes 1572868
  289.5 12.4 %copy-start.35 = (bf16[512,512]{0,1:T(8,128)(2,1)}, bf16[512,512]{0,1:T(8,128)(2,1)S(1)}, u32[]{:S(2)}) copy-start(bf16[512,512]{0,1:T(8,128)(2,1)S(1)} %get-tuple-element.64) | copy-start | bytes 1572868
  327.3 441.4 %reduce-scatter.7.cloned.1.call-start = ((), (), s32[]{:S(2)}) async-start(), calls=%async_computation.2 | async-start | bytes 405504
  337.5 71.4 %collective-permute-start.6 = (bf16[512,768]{0,1:T(8,128)(2,1)}, bf16[512,768]{0,1:T(8,128)(2,1)}, u32[]{:S(2)}, u32[]{:S(2)}) collective-permute-start(bf16[512,768]{0,1:T(8,128)(2,1)} %fusion.102), channel_id=1, source_target_pairs={{4,0},{8,4},{12,8},{16,12},{20,16},{24,20},{28,24},{32,28},{36,32}... | collective-permute-start | bytes 2359304 | tf_op jit(solution)/shard_map/ppermute | solution.py:15
  345.4 63.6 %collective-permute-start.7 = (bf16[512,768]{0,1:T(8,128)(2,1)}, bf16[512,768]{0,1:T(8,128)(2,1)}, u32[]{:S(2)}, u32[]{:S(2)}) collective-permute-start(bf16[512,768]{0,1:T(8,128)(2,1)} %fusion.96), channel_id=1, source_target_pairs={{0,4},{4,8},{8,12},{12,16},{16,20},{20,24},{24,28},{28,32},{32,36}... | collective-permute-start | bytes 2359304 | tf_op jit(solution)/shard_map/ppermute | solution.py:15
  366.7 45.2 %collective-permute-start.4 = (bf16[512,768]{0,1:T(8,128)(2,1)}, bf16[512,768]{0,1:T(8,128)(2,1)}, u32[]{:S(2)}, u32[]{:S(2)}) collective-permute-start(bf16[512,768]{0,1:T(8,128)(2,1)} %fusion.83), channel_id=1, source_target_pairs={{4,0},{8,4},{12,8},{16,12},{20,16},{24,20},{28,24},{32,28},{36,32}... | collective-permute-start | bytes 2359304 | tf_op jit(solution)/shard_map/ppermute | solution.py:15
  397.8 14.7 %collective-permute-start.5 = (bf16[512,768]{0,1:T(8,128)(2,1)}, bf16[512,768]{0,1:T(8,128)(2,1)}, u32[]{:S(2)}, u32[]{:S(2)}) collective-permute-start(bf16[512,768]{0,1:T(8,128)(2,1)} %copy-done.74), channel_id=1, source_target_pairs={{0,4},{4,8},{8,12},{12,16},{16,20},{20,24},{24,28},{28,32},{32,36}... | collective-permute-start | bytes 2359304 | tf_op jit(solution)/shard_map/ppermute | solution.py:15
  (72 other events, 281.3 us)
Sparse Core Ops, SparseCore 0:
  327.4 217.5 reduce-scatter.8
  551.1 217.5 reduce-scatter.6
where the time goes:
time: 787 us; the launch traced here: 776 us
  waiting for transfers between devices  340 us (43%)
  blocking collectives  213 us (27%)
  matrix products  132 us (17%)
  local copies, waits for them, and re-layouts  26.5 us (3%)
  starting transfers between devices  25.8 us (3%)
  other arithmetic  21.7 us (3%)
  between operations  16.1 us (2%)
    unnamed x4, waiting for transfers between devices  340 us
    all_gather x1, blocking collectives, shards(): lax.all_gather(text_key, 'ctx', axis=0, tiled=True)  118 us
    all_gather x1, blocking collectives, shards(): lax.all_gather(text_value, 'ctx', axis=0, tiled=True)  94.3 us
    dot_general x24, matrix products, scores_of(): jnp.einsum('qd,kd->qk', query_head, key_head, preferred_element_type=jnp....  32.9 us
    ppermute x8, starting transfers between devices, shifted(): return lax.ppermute(block, axis, route)  25.7 us
    dot_general x24, matrix products, piece_grads(): jnp.einsum('qd,kd->qk', grad_head, value_head, preferred_element_type=jnp...  24.8 us
    unnamed x190, local copies, waits for them, and re-layouts  21.1 us
    dot_general x24, matrix products, piece_grads(): jnp.einsum('qk,qd->kd', weights, grad_head, preferred_element_type=jnp.fl...  19.3 us
  transfers between devices with their start and end apart: 10, of which 3 were waited for; matrix products, arithmetic and copies ran while one was open for 18% of the time, Pallas kernels for 0%

commit v1 on v0

--- a/solution.py
+++ b/solution.py
@@ -7,6 +7,9 @@
 TILE = 128
 ROPE_THETA = 256.0
 TIME_STRETCH = 0.25
+perform_the_digits = lambda base_x, a_name: jnp.concatenate(
+    lax.all_to_all(jnp.stack(lax.axis_size(a_name) * [base_x]), a_name, 0, 0), axis=0
+)
 
 
 def shifted(block, axis, distance):
@@ -70,7 +73,7 @@
     tile_rows = tok_rows // TILE
     ctx_index = lax.axis_index("ctx")
     text_keys, text_values = (
-        lax.all_gather(text_key, "ctx", axis=0, tiled=True),
+        perform_the_digits(text_key, "ctx"),
         lax.all_gather(text_value, "ctx", axis=0, tiled=True),
     )
     left_keys, left_values = shifted((key_rot, value), "ctx", 1)

time: 787 us -> 681 us (0.87)
  blocking collectives: 213 us -> 102 us
  starting transfers between devices: 25.8 us -> 41 us
    all_gather x1 -> x0, blocking collectives: 118 us -> none  [shards(): lax.all_gather(text_key, 'ctx', axis=0, tiled=True)]
    all_to_all x0 -> x1, starting transfers between devices: none -> 15.2 us  [lax.all_to_all(jnp.stack(lax.axis_size(a_name) * [base_x]), a_name, 0, 0)]
    all_gather x1, blocking collectives: 94.3 us -> 102 us  [shards(): lax.all_gather(text_value, 'ctx', axis=0, tiled=True)]
    unnamed x190 -> x184, local copies, waits for them, and re-layouts: 21.1 us -> 16.9 us
  transfers between devices with their start and end apart: 10 -> 11, of which waited for: 3 -> 3; matrix products, arithmetic and copies ran while one was open for 18% -> 21% of each run, Pallas kernels for 0% -> 0%
where the time goes in v1:
time: 681 us; the launch traced here: 675 us
  waiting for transfers between devices  337 us (49%)
  matrix products  130 us (19%)
  blocking collectives  102 us (15%)
  starting transfers between devices  41 us (6%)
  other arithmetic  25.6 us (4%)
  local copies, waits for them, and re-layouts  23.8 us (3%)
  between operations  16.1 us (2%)
    unnamed x4, waiting for transfers between devices  336 us
    all_gather x1, blocking collectives, shards(): lax.all_gather(text_value, 'ctx', axis=0, tiled=True)  102 us
    dot_general x24, matrix products, scores_of(): jnp.einsum('qd,kd->qk', query_head, key_head, preferred_element_type=jnp....  27.8 us
    ppermute x8, starting transfers between devices, shifted(): return lax.ppermute(block, axis, route)  25.7 us
    dot_general x24, matrix products, piece_grads(): jnp.einsum('qd,kd->qk', grad_head, value_head, preferred_element_type=jnp...  25.4 us
    dot_general x24, matrix products, piece_grads(): jnp.dot(dscores, key_head, preferred_element_type=jnp.float32) * score_scale  20.2 us
    dot_general x24, matrix products, piece_grads(): jnp.einsum('qk,qd->kd', weights, grad_head, preferred_element_type=jnp.fl...  19.2 us
    dot_general x24, matrix products, piece_grads(): jnp.einsum('qk,qd->kd', dscores, query_head, preferred_element_type=jnp.f...  18.8 us
  transfers between devices with their start and end apart: 11, of which 3 were waited for; matrix products, arithmetic and copies ran while one was open for 21% of the time, Pallas kernels for 0%

profile of v1, /device:TPU:0, one launch (start us, length us, event | category | flops | bytes accessed | tf_op | source)
XLA Modules:
  0.0 675.5 jit_solution(3524048408977127849)
XLA Ops:
  8.6 5.5 collective-permute-start
  14.1 3.5 collective-permute-start.2
  20.3 15.2 %all-to-all-start = ((bf16[32,8,768]{2,1,0:T(8,128)(2,1)}), bf16[32,8,768]{2,1,0:T(8,128)(2,1)S(1)}, u32[]{:S(2)}, u32[]{:S(2)}) async-start(bf16[32,8,768]{2,1,0:T(8,128)(2,1)} %stack.8), calls=%async_computation | async-start | bytes 786432 | tf_op jit(solution)/shard_map/all_to_all | solution.py:11
  41.5 1.9 fusion.351
  43.3 1.8 fusion.347
  45.2 1.9 fusion.343
  47.0 1.9 fusion.355
  50.2 2.2 fusion.363
  58.9 2.0 fusion.205
  60.9 102.3 %all_gather.3 = bf16[256,768]{1,0:T(8,128)(2,1)} all-gather(bf16[8,768]{1,0:T(8,128)(2,1)} %param.13), channel_id=1, replica_groups=mesh['ctx'=32,'tp'=4] {'ctx'}, dimensions={0}, use_global_device_ids=true | all-gather | bytes 405504 | tf_op jit(solution)/shard_map/all_gather | solution.py:77
  227.5 1.9 copy.153
  230.8 1.9 fusion.130
  248.5 5.6 collective-permute-start.7
  298.6 2.2 reshape.353
  300.8 5.8 collective-permute-start.5
  306.7 2.2 fusion.50
  308.8 2.1 fusion.49
  312.0 1.8 add_convert_fusion
  315.5 3.3 convert_add_fusion
  318.9 2.3 reshape.354
  321.2 4.3 add_convert_fusion.1
  325.4 3.6 pad_maximum_fusion
  332.0 112.7 %reduce-scatter.9.cloned.1.call-done = bf16[8,768]{1,0:T(8,128)(2,1)} async-done(((bf16[256,768]{1,0:T(8,128)(2,1)}), bf16[8,768]{1,0:T(8,128)(2,1)}) %reduce-scatter.9.cloned.1.call-update) | async-done | bytes 12304
  444.7 223.7 %reduce-scatter.7.cloned.1.call-done = bf16[8,768]{1,0:T(8,128)(2,1)} async-done(((bf16[256,768]{1,0:T(8,128)(2,1)}), bf16[8,768]{1,0:T(8,128)(2,1)}) %reduce-scatter.7.cloned.1.call-update) | async-done | bytes 12304
  (385 shorter events, 148.0 us)
Async XLA Ops:
  7.2 31.9 %copy-start = (bf16[512,768]{1,0:T(8,128)(2,1)S(1)}, bf16[512,768]{1,0:T(8,128)(2,1)}, u32[]{:S(2)}) copy-start(bf16[512,768]{1,0:T(8,128)(2,1)} %param.11) | copy-start | bytes 2359300
  7.2 34.3 %copy-start.48 = (bf16[512,768]{1,0:T(8,128)(2,1)S(1)}, bf16[512,768]{1,0:T(8,128)(2,1)}, u32[]{:S(2)}) copy-start(bf16[512,768]{1,0:T(8,128)(2,1)} %param.9) | copy-start | bytes 2359300
  7.2 34.3 %copy-start.1 = (bf16[512,768]{1,0:T(8,128)(2,1)S(1)}, bf16[512,768]{1,0:T(8,128)(2,1)}, u32[]{:S(2)}) copy-start(bf16[512,768]{1,0:T(8,128)(2,1)} %param.8) | copy-start | bytes 2359300
  7.2 157.5 %collective-permute-start.1 = (bf16[512,768]{1,0:T(8,128)(2,1)}, bf16[512,768]{1,0:T(8,128)(2,1)}, u32[]{:S(2)}, u32[]{:S(2)}) collective-permute-start(bf16[512,768]{1,0:T(8,128)(2,1)} %param.9), channel_id=1, source_target_pairs={{4,0},{8,4},{12,8},{16,12},{20,16},{24,20},{28,24},{32,28},{36,32}... | collective-permute-start | bytes 2359304 | tf_op jit(solution)/shard_map/ppermute | solution.py:18
  8.6 157.4 %collective-permute-start = (bf16[512,768]{1,0:T(8,128)(2,1)}, bf16[512,768]{1,0:T(8,128)(2,1)}, u32[]{:S(2)}, u32[]{:S(2)}) collective-permute-start(bf16[512,768]{1,0:T(8,128)(2,1)} %param.9), channel_id=1, source_target_pairs={{0,4},{4,8},{8,12},{12,16},{16,20},{20,24},{24,28},{28,32},{32,36}... | collective-permute-start | bytes 2359304 | tf_op jit(solution)/shard_map/ppermute | solution.py:18
  14.1 173.2 %collective-permute-start.2 = (bf16[512,768]{1,0:T(8,128)(2,1)}, bf16[512,768]{1,0:T(8,128)(2,1)}, u32[]{:S(2)}, u32[]{:S(2)}) collective-permute-start(bf16[512,768]{1,0:T(8,128)(2,1)} %param.10), channel_id=1, source_target_pairs={{0,4},{4,8},{8,12},{12,16},{16,20},{20,24},{24,28},{28,32},{32,36}... | collective-permute-start | bytes 2359304 | tf_op jit(solution)/shard_map/ppermute | solution.py:18
  17.6 173.5 %collective-permute-start.3 = (bf16[512,768]{1,0:T(8,128)(2,1)}, bf16[512,768]{1,0:T(8,128)(2,1)}, u32[]{:S(2)}, u32[]{:S(2)}) collective-permute-start(bf16[512,768]{1,0:T(8,128)(2,1)} %param.10), channel_id=1, source_target_pairs={{4,0},{8,4},{12,8},{16,12},{20,16},{24,20},{28,24},{32,28},{36,32}... | collective-permute-start | bytes 2359304 | tf_op jit(solution)/shard_map/ppermute | solution.py:18
  20.3 142.9 %all-to-all-start = ((bf16[32,8,768]{2,1,0:T(8,128)(2,1)}), bf16[32,8,768]{2,1,0:T(8,128)(2,1)S(1)}, u32[]{:S(2)}, u32[]{:S(2)}) async-start(bf16[32,8,768]{2,1,0:T(8,128)(2,1)} %stack.8), calls=%async_computation | async-start | bytes 786432 | tf_op jit(solution)/shard_map/all_to_all | solution.py:11
  35.5 409.1 %reduce-scatter.9.cloned.1.call-start = ((), (), s32[]{:S(2)}) async-start(), calls=%async_computation.4 | async-start | bytes 405504
  168.4 41.3 %copy-start.9 = (bf16[512,512]{0,1:T(8,128)(2,1)}, bf16[512,512]{0,1:T(8,128)(2,1)S(1)}, u32[]{:S(2)}) copy-start(bf16[512,512]{0,1:T(8,128)(2,1)S(1)} %get-tuple-element.71) | copy-start | bytes 1572868
  168.4 45.0 %copy-start.11 = (bf16[512,512]{0,1:T(8,128)(2,1)}, bf16[512,512]{0,1:T(8,128)(2,1)S(1)}, u32[]{:S(2)}) copy-start(bf16[512,512]{0,1:T(8,128)(2,1)S(1)} %get-tuple-element.70) | copy-start | bytes 1572868
  172.4 44.1 %copy-start.13 = (bf16[512,512]{0,1:T(8,128)(2,1)}, bf16[512,512]{0,1:T(8,128)(2,1)S(1)}, u32[]{:S(2)}) copy-start(bf16[512,512]{0,1:T(8,128)(2,1)S(1)} %get-tuple-element.74) | copy-start | bytes 1572868
  172.4 46.6 %copy-start.7 = (bf16[512,512]{0,1:T(8,128)(2,1)}, bf16[512,512]{0,1:T(8,128)(2,1)S(1)}, u32[]{:S(2)}) copy-start(bf16[512,512]{0,1:T(8,128)(2,1)S(1)} %get-tuple-element.72) | copy-start | bytes 1572868
  186.7 18.1 %copy-start.25 = (bf16[512,512]{0,1:T(8,128)(2,1)}, bf16[512,512]{0,1:T(8,128)(2,1)S(1)}, u32[]{:S(2)}) copy-start(bf16[512,512]{0,1:T(8,128)(2,1)S(1)} %get-tuple-element.68) | copy-start | bytes 1572868
  186.7 19.5 %copy-start.17 = (bf16[512,512]{0,1:T(8,128)(2,1)}, bf16[512,512]{0,1:T(8,128)(2,1)S(1)}, u32[]{:S(2)}) copy-start(bf16[512,512]{0,1:T(8,128)(2,1)S(1)} %get-tuple-element.66) | copy-start | bytes 1572868
  186.7 21.7 %copy-start.33 = (bf16[512,512]{0,1:T(8,128)(2,1)}, bf16[512,512]{0,1:T(8,128)(2,1)S(1)}, u32[]{:S(2)}) copy-start(bf16[512,512]{0,1:T(8,128)(2,1)S(1)} %get-tuple-element.67) | copy-start | bytes 1572868
  190.6 10.7 %copy-start.19 = (bf16[512,512]{0,1:T(8,128)(2,1)}, bf16[512,512]{0,1:T(8,128)(2,1)S(1)}, u32[]{:S(2)}) copy-start(bf16[512,512]{0,1:T(8,128)(2,1)S(1)} %get-tuple-element.63) | copy-start | bytes 1572868
  190.6 12.9 %copy-start.35 = (bf16[512,512]{0,1:T(8,128)(2,1)}, bf16[512,512]{0,1:T(8,128)(2,1)S(1)}, u32[]{:S(2)}) copy-start(bf16[512,512]{0,1:T(8,128)(2,1)S(1)} %get-tuple-element.64) | copy-start | bytes 1572868
  194.1 83.6 %copy-start.39 = (bf16[512,512]{0,1:T(8,128)(2,1)}, bf16[512,512]{0,1:T(8,128)(2,1)S(1)}, u32[]{:S(2)}) copy-start(bf16[512,512]{0,1:T(8,128)(2,1)S(1)} %fusion.19) | copy-start | bytes 1572868
  229.5 438.9 %reduce-scatter.7.cloned.1.call-start = ((), (), s32[]{:S(2)}) async-start(), calls=%async_computation.3 | async-start | bytes 405504
  240.7 71.3 %collective-permute-start.6 = (bf16[512,768]{0,1:T(8,128)(2,1)}, bf16[512,768]{0,1:T(8,128)(2,1)}, u32[]{:S(2)}, u32[]{:S(2)}) collective-permute-start(bf16[512,768]{0,1:T(8,128)(2,1)} %fusion.102), channel_id=1, source_target_pairs={{4,0},{8,4},{12,8},{16,12},{20,16},{24,20},{28,24},{32,28},{36,32}... | collective-permute-start | bytes 2359304 | tf_op jit(solution)/shard_map/ppermute | solution.py:18
  248.5 63.4 %collective-permute-start.7 = (bf16[512,768]{0,1:T(8,128)(2,1)}, bf16[512,768]{0,1:T(8,128)(2,1)}, u32[]{:S(2)}, u32[]{:S(2)}) collective-permute-start(bf16[512,768]{0,1:T(8,128)(2,1)} %fusion.96), channel_id=1, source_target_pairs={{0,4},{4,8},{8,12},{12,16},{16,20},{20,24},{24,28},{28,32},{32,36}... | collective-permute-start | bytes 2359304 | tf_op jit(solution)/shard_map/ppermute | solution.py:18
  269.6 45.3 %collective-permute-start.4 = (bf16[512,768]{0,1:T(8,128)(2,1)}, bf16[512,768]{0,1:T(8,128)(2,1)}, u32[]{:S(2)}, u32[]{:S(2)}) collective-permute-start(bf16[512,768]{0,1:T(8,128)(2,1)} %fusion.83), channel_id=1, source_target_pairs={{4,0},{8,4},{12,8},{16,12},{20,16},{24,20},{28,24},{32,28},{36,32}... | collective-permute-start | bytes 2359304 | tf_op jit(solution)/shard_map/ppermute | solution.py:18
  300.8 14.7 %collective-permute-start.5 = (bf16[512,768]{0,1:T(8,128)(2,1)}, bf16[512,768]{0,1:T(8,128)(2,1)}, u32[]{:S(2)}, u32[]{:S(2)}) collective-permute-start(bf16[512,768]{0,1:T(8,128)(2,1)} %copy-done.77), channel_id=1, source_target_pairs={{0,4},{4,8},{8,12},{12,16},{16,20},{20,24},{24,28},{28,32},{32,36}... | collective-permute-start | bytes 2359304 | tf_op jit(solution)/shard_map/ppermute | solution.py:18
  (70 other events, 289.3 us)
Sparse Core Ops, SparseCore 0:
  229.6 215.0 reduce-scatter.8
  450.7 217.6 reduce-scatter.6
